TPU v7x, 128 devices: a whole 4x4x4 slice. The times are simulated.
128 devices in a mesh: section: 2 (over x_lo), rows: 8 (over y, x_hi), chan: 8 (over z, core).
Axes of the slice: x: 4 (x_hi: 2, x_lo: 2; x = x_hi * 2 + x_lo), y: 4, z: 4, core: 2. Of those that a mesh axis runs over, the one named last changes fastest.
Arguments:
- condition: float32 [12, 128, 1024], P(None, 'rows'), may hold values from -6 to 6
- target: float32 [12, 128, 1024], P(None, 'rows'), may hold values from -6 to 6
- noise_draw: float32 [12, 128, 1024], P(None, 'rows'), may hold values from -6 to 6
- sigma_index: int32 [1], replicated, may hold values from 0 to 31
- reg_first: bfloat16 [3, 3, 12, 128], P(None, None, None, 'chan'), may hold values from -0.625 to 0.625
- reg_second: bfloat16 [3, 3, 128, 12], P(None, None, 'chan'), may hold values from -0.1875 to 0.1875
- first_kernel: bfloat16 [3, 3, 24, 128], P(None, None, None, ('section', 'chan')), may hold values from -0.4375 to 0.4375
- second_kernel: bfloat16 [3, 3, 128, 128], P(None, None, None, ('section', 'chan')), may hold values from -0.1875 to 0.1875
- third_kernel: bfloat16 [3, 3, 128, 12], P(None, None, ('section', 'chan')), may hold values from -0.1875 to 0.1875
- film_scale: bfloat16 [128], P(('section', 'chan')), may hold values from -4 to 4
Outputs:
- denoised: bfloat16 [12, 128, 1024], P(None, 'rows')
- grad_first: float32 [3, 3, 24, 128], P(None, None, None, ('section', 'chan'))
- grad_second: float32 [3, 3, 128, 128], P(None, None, None, ('section', 'chan'))
- grad_third: float32 [3, 3, 128, 12], P(None, None, ('section', 'chan'))
- grad_film: float32 [128], P(('section', 'chan'))
Inputs may be any that keep to these rules, and one draw needn't show every extreme that they name: `sigma_index`: an index into the table of 32 noise levels.
All inputs are finite; a program needn't handle non-finite values.
Results may differ from a plain program's by a relative error of at most 0.008.
Values may be sent and summed in bfloat16 or wider, within the bound.
No kernel may reach another device: no remote copies, remote signals or barrier semaphores. Data moves between devices by JAX's collectives and lax.ppermute only.
A program may use at most 128 MiB of HBM per device.

v0:
```python
import math
import jax
import jax.numpy as jnp
from jax import lax
from jax.sharding import PartitionSpec as P

COUT = 12
NSIG = 32
sigma_low = 0.25
sigma_high = 4.0
rho_power = 7.0
sigma_data = 0.5


def padded(array, sides, width):
    for axis, dim in sides:
        size, length = (lax.axis_size(axis), array.shape[dim])
        up = [(i, (i + 1) % size) for i in range(size - 1)]
        down = [(j, i) for i, j in up]
        last = lax.slice_in_dim(array, length - width, length, axis=dim)
        leading = lax.slice_in_dim(array, 0, width, axis=dim)
        before = lax.ppermute(last, axis, up)
        after = lax.ppermute(leading, axis, down)
        array = jnp.concatenate([before, array, after], axis=dim)
    return array


def noise_terms(sigma_index):
    steps_at = jnp.arange(NSIG, dtype=jnp.float32) / (NSIG - 1)
    high_root = sigma_high ** (1.0 / rho_power)
    low_root = sigma_low ** (1.0 / rho_power)
    levels = (high_root + steps_at * (low_root - high_root)) ** rho_power
    picked = jnp.arange(NSIG, dtype=jnp.int32) == sigma_index[0]
    sigma_level = jnp.sum(jnp.where(picked, levels, jnp.zeros_like(levels)))
    total_var = sigma_level * sigma_level + sigma_data * sigma_data
    skip_coef = sigma_data * sigma_data / total_var
    out_coef = sigma_level * sigma_data / jnp.sqrt(total_var)
    in_coef = 1.0 / jnp.sqrt(total_var)
    noise_coef = jnp.log(8.0 * sigma_level) / 4.0
    loss_weight = total_var / (sigma_level * sigma_data) ** 2
    return (sigma_level, skip_coef, out_coef, in_coef, noise_coef, loss_weight)


def conv_rows(grid_field, kernel):
    result_conv = lax.conv_general_dilated(
        grid_field[None],
        kernel,
        (1, 1),
        ((0, 0), (1, 1)),
        dimension_numbers=("NCHW", "HWIO", "NCHW"),
        preferred_element_type=jnp.float32,
    )
    return result_conv[0]


def kernel_grad(grid_field, delta_in):
    result_conv = lax.conv_general_dilated(
        grid_field[:, None],
        delta_in[:, None],
        (1, 1),
        ((0, 0), (1, 1)),
        dimension_numbers=("NCHW", "OIHW", "NCHW"),
        preferred_element_type=jnp.float32,
    )
    return jnp.transpose(result_conv, (2, 3, 0, 1))


def turned(kernel):
    return jnp.transpose(jnp.flip(kernel, (0, 1)), (0, 1, 3, 2))


def silu_slope(pre_act):
    sigmoid_at = jax.nn.sigmoid(pre_act)
    return sigmoid_at * (1.0 + pre_act * (1.0 - sigmoid_at))


def grid_rows(grid_field, first_row, total_rows):
    places = first_row + jnp.arange(grid_field.shape[1], dtype=jnp.int32)
    inside = (places >= 0) & (places < total_rows)
    return jnp.where(inside[None, :, None], grid_field, jnp.zeros_like(grid_field))


def shards(
    condition,
    target,
    noise_draw,
    sigma_index,
    reg_first,
    reg_second,
    first_kernel,
    second_kernel,
    third_kernel,
    film_scale,
):
    rows_dev = condition.shape[1]
    grid_width = condition.shape[2]
    total_rows = rows_dev * lax.axis_size("rows")
    slab_start = lax.axis_index("rows") * rows_dev
    section_id = lax.axis_index("section")
    member = lax.axis_index(("section", "chan"))
    local_ch = film_scale.shape[0]
    sigma_level, skip_coef, out_coef, in_coef, noise_coef, loss_weight = noise_terms(sigma_index)
    grad_scale = 1.0 / math.sqrt(COUT * total_rows * grid_width)
    cond_low = condition.astype(jnp.bfloat16)
    cond_rim = padded(cond_low, (("rows", 1),), 2)
    half_rows = rows_dev // lax.axis_size("section")
    half_start = section_id * half_rows
    reg_input = lax.dynamic_slice_in_dim(cond_rim, half_start, half_rows + 4, 1)
    reg_hidden = jax.nn.silu(conv_rows(reg_input, reg_first))
    reg_hidden = grid_rows(reg_hidden, slab_start + half_start - 1, total_rows).astype(jnp.bfloat16)
    mean_part = conv_rows(reg_hidden, reg_second)
    mean_half = lax.psum(mean_part, "chan").astype(jnp.bfloat16)
    mean_field = lax.all_gather(mean_half, "section", axis=1, tiled=True)
    resid_field = target - mean_field.astype(jnp.float32)
    noisy_field = resid_field + sigma_level * noise_draw
    scaled_in = (in_coef * noisy_field).astype(jnp.bfloat16)
    film_gain = 1.0 + noise_coef * film_scale.astype(jnp.float32)
    input_rim = padded(scaled_in, (("rows", 1),), 2)
    stacked = jnp.concatenate([input_rim, cond_rim], 0)
    whole_first, whole_film = (
        lax.all_gather(first_kernel, ("section", "chan"), axis=3, tiled=True),
        lax.all_gather(film_scale, ("section", "chan"), axis=0, tiled=True),
    )
    first_all = conv_rows(stacked, whole_first)
    gain_all = (1.0 + noise_coef * whole_film.astype(jnp.float32))[:, None, None]
    hidden_full = grid_rows(jax.nn.silu(first_all * gain_all), slab_start - 1, total_rows).astype(
        jnp.bfloat16
    )
    first_mine = lax.dynamic_slice_in_dim(first_all, member * local_ch, local_ch, 0)[:, 1:-1]
    second_act = conv_rows(hidden_full, second_kernel)
    second_hidden = jax.nn.silu(second_act).astype(jnp.bfloat16)
    second_rim = padded(second_hidden, (("rows", 1),), 1)
    out_part = conv_rows(second_rim, third_kernel)
    out_full = lax.psum(out_part, ("section", "chan"))
    den_value = skip_coef * noisy_field + out_coef * out_full
    out_delta = (2.0 * loss_weight * out_coef * grad_scale * (den_value - resid_field)).astype(
        jnp.bfloat16
    )
    out_delta_rim = padded(out_delta, (("rows", 1),), 1)
    grad_third = kernel_grad(second_rim, out_delta)
    second_delta = (conv_rows(out_delta_rim, turned(third_kernel)) * silu_slope(second_act)).astype(
        jnp.bfloat16
    )
    second_delta_rim = padded(second_delta, (("rows", 1),), 1)
    grad_second = kernel_grad(hidden_full, second_delta)
    whole_second = lax.all_gather(second_kernel, ("section", "chan"), axis=3, tiled=True)
    mine_second = turned(lax.dynamic_slice_in_dim(whole_second, member * local_ch, local_ch, 2))
    empty_sum = jnp.zeros((local_ch, rows_dev, grid_width), jnp.float32)
    shard_part = lax.all_gather(second_delta_rim, ("section", "chan"), axis=0, tiled=True)
    kernel_part = lax.slice_in_dim(mine_second, 0, shard_part.shape[0], axis=2)
    back_first = empty_sum + conv_rows(shard_part, kernel_part)
    gain_mine = film_gain[:, None, None]
    first_grad = back_first * silu_slope(first_mine * gain_mine)
    grad_film = noise_coef * jnp.sum(first_grad * first_mine, axis=(1, 2))
    first_delta = (first_grad * gain_mine).astype(jnp.bfloat16)
    grad_first = kernel_grad(stacked[:, 1:-1], first_delta)
    grad_parts = (grad_first, grad_second, grad_third, grad_film)
    den_out = den_value.astype(jnp.bfloat16)
    grad_first, grad_second, grad_third, grad_film = lax.psum(
        (grad_parts[0], grad_parts[1], grad_parts[2], grad_parts[3]), "rows"
    )
    return (den_out, grad_first, grad_second, grad_third, grad_film)


def solution(mesh):
    return jax.shard_map(
        shards,
        mesh=mesh,
        in_specs=(
            P(None, "rows", None),
            P(None, "rows", None),
            P(None, "rows", None),
            P(),
            P(None, None, None, "chan"),
            P(None, None, "chan", None),
            P(None, None, None, ("section", "chan")),
            P(None, None, None, ("section", "chan")),
            P(None, None, ("section", "chan"), None),
            P(("section", "chan")),
        ),
        out_specs=(
            P(None, "rows", None),
            P(None, None, None, ("section", "chan")),
            P(None, None, None, ("section", "chan")),
            P(None, None, ("section", "chan"), None),
            P(("section", "chan")),
        ),
        check_vma=False,
    )
```

profile of v0, /device:TPU:0, one launch (start us, length us, event | category | flops | bytes accessed | tf_op | source)
XLA Modules:
  0.0 844.1 jit_solution(11145103124998721474)
XLA Ops:
  18.9 30.4 %all-reduce = bf16[128]{0:T(256)(128)(2,1)S(1)} all-reduce(bf16[128]{0:T(256)(128)(2,1)S(1)} %dynamic-update-slice), channel_id=1, replica_groups=mesh['section'=2,'rows'=8,'chan'=8] {'section','chan'}, use_global_device_ids=true, to_apply=%add | all-reduce | flops 128 | bytes 512
  58.5 7.3 select_bitcast_fusion.1
  75.3 27.6 %all-reduce.6 = bf16[12,8,1024]{2,1,0:T(8,128)(2,1)S(1)} all-reduce(f32[12,8,1024]{2,1,0:T(8,128)S(1)} %slice_bitcast_fusion.3), channel_id=1, replica_groups=mesh['section'=2,'rows'=8,'chan'=8] {'chan'}, use_global_device_ids=true, to_apply=%region_1.2 | all-reduce | flops 98304 | bytes 589824 | tf_op jit(solution)/shard_map/psum | solution.py:112
  112.7 7.0 collective-permute-start.2
  119.8 18.4 %all_gather.16 = bf16[3,3,24,128]{2,3,1,0:T(8,128)(2,1)S(1)} all-gather(bf16[3,3,24,8]{2,3,1,0:T(8,128)(2,1)S(1)} %copy-done.8), channel_id=1, replica_groups=mesh['section'=2,'rows'=8,'chan'=8] {'section','chan'}, dimensions={3}, use_global_device_ids=true | all-gather | bytes 58752 | tf_op jit(solution)/shard_map/all_gather | solution.py:121
  150.9 8.9 %broadcast_select_fusion = f32[18,8,129,128]{3,1,2,0:T(8,128)S(1)} fusion(pred[8,129]{0,1:T(8,128)(4,1)S(1)} %copy-done.10, bf16[3,3,24,128]{2,3,1,0:T(8,128)(2,1)S(1)} %all_gather.16, bf16[24,20,1,7,2]{0,3,4,1,2:T(8,128)(2,1)S(1)} %slice.71, bf16[24,20,1,8,129]{0,3,4,1,2:T(8,128)(2,1)} %copy.92), kind=kOutput, calls=%fused_computation.56 | convolution fusion | flops 1032574464 | bytes 10571400 | tf_op jit(solution)/shard_map/conv_general_dilated | solution.py:45
  163.7 12.6 %fusion.30 = f32[16,8,129,8]{3,1,2,0:T(8,128)} fusion(bf16[3,3,128,8]{2,3,1,0:T(8,128)(2,1)S(1)} %copy-done.9, bf16[18,1,7,1,128]{4,2,3,0,1:T(8,128)(2,1)S(1)} %get-tuple-element.17, bf16[18,1,7,1,128]{4,2,3,0,1:T(8,128)(2,1)S(1)} %get-tuple-element.16, bf16[18,1,8,129,128]{4,2,3,0,1:T(8,128)(2,1)S(1)} %select_bitcast_fusion), kind=kOutput, calls=%fused_computation.39 | convolution fusion | flops 328495104 | bytes 5366784 | tf_op jit(solution)/shard_map/conv_general_dilated | solution.py:45
  185.0 7.3 collective-permute-start.4
  192.3 18.4 %all_gather.19 = bf16[3,3,128,128]{2,3,1,0:T(8,128)(2,1)} all-gather(bf16[3,3,128,8]{2,3,1,0:T(8,128)(2,1)S(1)} %copy-done.9), channel_id=1, replica_groups=mesh['section'=2,'rows'=8,'chan'=8] {'section','chan'}, dimensions={3}, use_global_device_ids=true | all-gather | bytes 313344 | tf_op jit(solution)/shard_map/all_gather | solution.py:146
  211.5 18.9 %copy.120 = f32[18,8,129,128]{2,1,3,0:T(8,128)} copy(f32[18,8,129,128]{3,1,2,0:T(8,128)} %copy-done.2) | data formatting | bytes 19021824 | tf_op jit(solution)/shard_map/conv_general_dilated | solution.py:45
  230.4 17.9 %reshape.184 = f32[18,1,1032,128]{2,3,0,1:T(8,128)} reshape(f32[18,8,129,128]{2,1,3,0:T(8,128)} %copy.120) | data formatting | bytes 19021824 | tf_op jit(solution)/shard_map/conv_general_dilated | solution.py:45
  255.9 11.2 %broadcast_select_fusion.3 = f32[16,8,129,12]{3,1,2,0:T(8,128)} fusion(pred[8,129]{0,1:T(8,128)(4,1)S(1)} %copy-done.10, bf16[3,3,8,12]{3,2,1,0:T(8,128)(2,1)S(1)} %copy-done.13, bf16[8,18,1,7,2]{0,3,4,1,2:T(8,128)(2,1)S(1)} %slice.77, bf16[8,18,1,8,129]{0,3,4,1,2:T(8,128)(2,1)} %copy.95), kind=kOutput, calls=%fused_computation.59 | convolution fusion | flops 29636352 | bytes 1096584 | tf_op jit(solution)/shard_map/conv_general_dilated | solution.py:45
  267.0 8.0 copy.96
  278.2 8.4 %select_convert_fusion.1 = bf16[128,1,18,1024]{3,0,2,1:T(8,128)(2,1)} fusion(f32[128]{0:T(128)S(1)} %multiply_add_fusion.3, pred[18]{0:T(512)(128)(4,1)S(1)} %compare_and_fusion, f32[18,1,1032,128]{2,3,0,1:T(8,128)} %reshape.184), kind=kLoop, calls=%fused_computation.14 | loop fusion | flops 16515072 | bytes 14156306 | tf_op jit(solution)/shard_map/convert_element_type | solution.py:126
  287.3 111.4 %all-reduce.5.cloned.1.call-done = f32[12,16,1024]{2,1,0:T(8,128)} async-done(((f32[12,16,1024]{2,1,0:T(8,128)}), f32[12,16,1024]{2,1,0:T(8,128)}) %all-reduce.5.cloned.1.call-update) | async-done | bytes 786448 | tf_op jit(solution)/shard_map/psum | solution.py:134
  410.0 9.3 %slice.88 = f32[18,1,1024,128]{2,3,0,1:T(8,128)} slice(f32[18,1,1032,128]{2,3,0,1:T(8,128)} %reshape.184), slice={[0:18], [0:1], [0:1024], [0:128]} | slice | bytes 18874368 | tf_op jit(solution)/shard_map/conv_general_dilated | solution.py:45
  429.1 11.0 %broadcast_select_fusion.2 = f32[16,8,129,8]{3,1,2,0:T(8,128)} fusion(pred[8,129]{0,1:T(8,128)(4,1)S(1)} %copy-done.10, bf16[3,3,8,12]{3,2,1,0:T(8,128)(2,1)S(1)} %copy-done.13, bf16[12,18,1,7,2]{0,3,4,1,2:T(8,128)(2,1)S(1)} %slice.82, bf16[12,18,1,8,129]{0,3,4,1,2:T(8,128)(2,1)} %copy.99), kind=kOutput, calls=%fused_computation.58 | convolution fusion | flops 30023040 | bytes 983016 | tf_op jit(solution)/shard_map/conv_general_dilated | solution.py:45
  440.1 7.5 copy.100
  458.8 13.2 %copy.108 = bf16[24,1,18,1024]{0,1,3,2:T(2,128)(2,1)} copy(bf16[24,1,18,1024]{3,2,0,1:T(8,128)(2,1)S(1)} %slice_bitcast_fusion) | data formatting | bytes 1769472 | tf_op jit(solution)/shard_map/broadcast_in_dim | solution.py:58
  472.1 21.3 %copy.110 = bf16[128,1,18,1024]{0,1,3,2:T(2,128)(2,1)} copy(bf16[128,1,18,1024]{3,0,2,1:T(8,128)(2,1)} %select_convert_fusion.1) | data formatting | bytes 9437184 | tf_op jit(solution)/shard_map/convert_element_type | solution.py:126
  493.4 15.4 %copy.112 = bf16[8,1,18,1024]{0,1,3,2:T(2,128)(2,1)} copy(bf16[8,1,18,1024]{3,0,2,1:T(8,128)(2,1)S(1)} %copy-done.6) | data formatting | bytes 589824 | tf_op jit(solution)/shard_map/broadcast_in_dim | solution.py:58
  508.8 9.0 %copy.113 = bf16[12,1,16,1024]{0,1,3,2:T(2,128)(2,1)} copy(bf16[12,1,16,1024]{3,2,0,1:T(8,128)(2,1)S(1)} %bitcast.183) | data formatting | bytes 786432 | tf_op jit(solution)/shard_map/broadcast_in_dim | solution.py:59
  518.6 52.5 %fusion.140 = f32[3,3,8,12]{3,2,1,0:T(8,128)S(1)} fusion(bf16[8,1,18,1024]{0,1,3,2:T(2,128)(2,1)} %copy.112, bf16[12,1,16,1024]{0,1,3,2:T(2,128)(2,1)} %copy.113), kind=kOutput, calls=%fused_computation.171 | convolution fusion | flops 28293120 | bytes 691584 | tf_op jit(solution)/shard_map/transpose | solution.py:65
  571.3 14.2 %copy.111 = bf16[8,1,16,1024]{0,1,3,2:T(2,128)(2,1)} copy(bf16[8,1,16,1024]{3,0,2,1:T(8,128)(2,1)S(1)} %fusion.84) | data formatting | bytes 524288 | tf_op jit(solution)/shard_map/convert_element_type | solution.py:141
  585.5 66.0 %fusion.139 = f32[3,3,128,8]{2,3,1,0:T(8,128)S(1)} fusion(bf16[128,1,18,1024]{0,1,3,2:T(2,128)(2,1)} %copy.110, bf16[8,1,16,1024]{0,1,3,2:T(2,128)(2,1)} %copy.111), kind=kOutput, calls=%fused_computation.170 | convolution fusion | flops 301793280 | bytes 5017600 | tf_op jit(solution)/shard_map/transpose | solution.py:65
  651.5 7.7 pad.12
  659.1 17.5 %reshape.183 = bf16[128,18,1,8,129]{4,3,0,1,2:T(8,128)(2,1)} reshape(bf16[128,18,1,1032]{3,0,1,2:T(8,128)(2,1)} %pad.12) | data formatting | bytes 9510912 | tf_op jit(solution)/shard_map/conv_general_dilated | solution.py:45
  676.6 13.1 %copy.103 = bf16[128,18,1,8,129]{0,3,4,1,2:T(8,128)(2,1)} copy(bf16[128,18,1,8,129]{4,3,0,1,2:T(8,128)(2,1)} %reshape.183) | data formatting | bytes 9510912 | tf_op jit(solution)/shard_map/conv_general_dilated | solution.py:45
  690.7 14.4 %broadcast_select_fusion.1 = f32[16,8,129,8]{3,1,2,0:T(8,128)} fusion(pred[8,129]{0,1:T(8,128)(4,1)S(1)} %copy-done.10, bf16[128,18,1,7,2]{0,3,4,1,2:T(8,128)(2,1)S(1)} %slice.86, bf16[128,18,1,8,129]{0,3,4,1,2:T(8,128)(2,1)} %copy.103, bf16[3,3,128,128]{2,3,1,0:T(8,128)(2,1)S(1)} %copy-done.7, s32[]{:T(128)S(6)} %select_n.34), kind=kOutput, calls=%fused_computation.57 | convolution fusion | flops 318968832 | bytes 5644300 | tf_op jit(solution)/shard_map/conv_general_dilated | solution.py:45
  712.9 14.2 %copy.109 = bf16[8,1,16,1024]{0,1,3,2:T(2,128)(2,1)} copy(bf16[8,1,16,1024]{3,0,2,1:T(8,128)(2,1)S(1)} %fusion.101) | data formatting | bytes 524288 | tf_op jit(solution)/shard_map/broadcast_in_dim | solution.py:59
  727.1 66.0 %fusion.138 = f32[3,3,24,8]{2,3,1,0:T(8,128)S(1)} fusion(bf16[24,1,18,1024]{0,1,3,2:T(2,128)(2,1)} %copy.108, bf16[8,1,16,1024]{0,1,3,2:T(2,128)(2,1)} %copy.109), kind=kOutput, calls=%fused_computation.169 | convolution fusion | flops 56586240 | bytes 1153792 | tf_op jit(solution)/shard_map/transpose | solution.py:65
  793.1 43.7 %all-reduce.1 = (f32[3,3,24,8]{2,3,1,0:T(8,128)}, f32[3,3,128,8]{2,3,1,0:T(8,128)}, f32[3,3,8,12]{3,2,1,0:T(8,128)}, f32[8]{0:T(128)}) all-reduce(f32[3,3,24,8]{2,3,1,0:T(8,128)S(1)} %fusion.138, f32[3,3,128,8]{2,3,1,0:T(8,128)S(1)} %fusion.139, ...), channel_id=1, replica_groups=mesh['section'=2,'rows'=8,'chan'=8] {'rows'}, use_global_device_ids=true, to_apply=%region_3.4 | all-reduce | flops 11816 | bytes 94528 | tf_op jit(solution)/shard_map/psum | solution.py:159
  (113 shorter events, 115.3 us)
Async XLA Ops:
  7.2 51.3 %copy-start = (bf16[3,3,12,16]{3,2,1,0:T(8,128)(2,1)S(1)}, bf16[3,3,12,16]{3,2,1,0:T(8,128)(2,1)}, u32[]{:S(2)}) copy-start(bf16[3,3,12,16]{3,2,1,0:T(8,128)(2,1)} %param.14) | copy-start | bytes 10372
  7.2 51.3 %copy-start.10 = (pred[8,129]{0,1:T(8,128)(4,1)S(1)}, pred[8,129]{0,1:T(8,128)(4,1)}, u32[]{:S(2)}) copy-start(pred[8,129]{0,1:T(8,128)(4,1)} %constant.100) | copy-start | bytes 3100
  7.2 391.5 %all-reduce.5.cloned.1.call-start = ((), (), s32[]{:S(2)}) async-start(), calls=%async_computation | async-start | bytes 1572864 | tf_op jit(solution)/shard_map/psum | solution.py:134
  8.5 44.0 %collective-permute-start = (bf16[12,2,1024]{2,1,0:T(2,128)(2,1)S(1)}, bf16[12,2,1024]{2,1,0:T(2,128)(2,1)S(1)}, u32[]{:S(2)}, u32[]{:S(2)}) collective-permute-start(bf16[12,2,1024]{2,1,0:T(2,128)(2,1)S(1)} %get-tuple-element.26), channel_id=1, source_target_pairs={{0,8},{8,16},{16,24},{24,32},{32,40},{40,48},{48,56},{1,9},{9,17},... | collective-permute-start | bytes 147464 | tf_op jit(solution)/shard_map/ppermute | solution.py:22
  13.5 39.0 %collective-permute-start.1 = (bf16[12,2,1024]{2,1,0:T(2,128)(2,1)S(1)}, bf16[12,2,1024]{2,1,0:T(2,128)(2,1)S(1)}, u32[]{:S(2)}, u32[]{:S(2)}) collective-permute-start(bf16[12,2,1024]{2,1,0:T(2,128)(2,1)S(1)} %get-tuple-element.27), channel_id=1, source_target_pairs={{8,0},{16,8},{24,16},{32,24},{40,32},{48,40},{56,48},{9,1},{17,9},... | collective-permute-start | bytes 147464 | tf_op jit(solution)/shard_map/ppermute | solution.py:23
  58.5 7.4 copy-start.12
  70.7 38.6 %copy-start.4 = (f32[12,16,1024]{2,1,0:T(8,128)S(1)}, f32[12,16,1024]{2,1,0:T(8,128)}, u32[]{:S(2)}) copy-start(f32[12,16,1024]{2,1,0:T(8,128)} %param.11) | copy-start | bytes 2359300
  70.7 49.0 %copy-start.8 = (bf16[3,3,24,8]{2,3,1,0:T(8,128)(2,1)S(1)}, bf16[3,3,24,8]{2,3,1,0:T(8,128)(2,1)}, u32[]{:S(2)}) copy-start(bf16[3,3,24,8]{2,3,1,0:T(8,128)(2,1)} %param.16) | copy-start | bytes 10372
  109.3 28.8 %copy-start.3 = (bf16[12,16,1024]{2,1,0:T(8,128)(2,1)}, bf16[12,16,1024]{2,1,0:T(8,128)(2,1)S(1)}, u32[]{:S(2)}) copy-start(bf16[12,16,1024]{2,1,0:T(8,128)(2,1)S(1)} %all_gather.15) | copy-start | bytes 1179652
  111.4 26.7 %collective-permute-start.3 = (bf16[12,2,1024]{2,1,0:T(2,128)(2,1)S(1)}, bf16[12,2,1024]{2,1,0:T(2,128)(2,1)S(1)}, u32[]{:S(2)}, u32[]{:S(2)}) collective-permute-start(bf16[12,2,1024]{2,1,0:T(2,128)(2,1)S(1)} %get-tuple-element.25), channel_id=1, source_target_pairs={{8,0},{16,8},{24,16},{32,24},{40,32},{48,40},{56,48},{9,1},{17,9},... | collective-permute-start | bytes 147464 | tf_op jit(solution)/shard_map/ppermute | solution.py:23
  112.7 25.4 %collective-permute-start.2 = (bf16[12,2,1024]{2,1,0:T(2,128)(2,1)S(1)}, bf16[12,2,1024]{2,1,0:T(2,128)(2,1)S(1)}, u32[]{:S(2)}, u32[]{:S(2)}) collective-permute-start(bf16[12,2,1024]{2,1,0:T(2,128)(2,1)S(1)} %get-tuple-element.24), channel_id=1, source_target_pairs={{0,8},{8,16},{16,24},{24,32},{32,40},{40,48},{48,56},{1,9},{9,17},... | collective-permute-start | bytes 147464 | tf_op jit(solution)/shard_map/ppermute | solution.py:22
  159.7 3.9 copy-start.2
  159.8 3.9 copy-start.9
  183.7 64.6 %collective-permute-start.5 = (bf16[8,1,1024]{2,0,1:T(8,128)(2,1)S(1)}, bf16[8,1,1024]{2,0,1:T(8,128)(2,1)S(1)}, u32[]{:S(2)}, u32[]{:S(2)}) collective-permute-start(bf16[8,1,1024]{2,0,1:T(8,128)(2,1)S(1)} %get-tuple-element.33), channel_id=1, source_target_pairs={{8,0},{16,8},{24,16},{32,24},{40,32},{48,40},{56,48},{9,1},{17,9},... | collective-permute-start | bytes 49160 | tf_op jit(solution)/shard_map/ppermute | solution.py:23
  185.0 63.3 %collective-permute-start.4 = (bf16[8,1,1024]{2,0,1:T(8,128)(2,1)S(1)}, bf16[8,1,1024]{2,0,1:T(8,128)(2,1)S(1)}, u32[]{:S(2)}, u32[]{:S(2)}) collective-permute-start(bf16[8,1,1024]{2,0,1:T(8,128)(2,1)S(1)} %get-tuple-element.32), channel_id=1, source_target_pairs={{0,8},{8,16},{16,24},{24,32},{32,40},{40,48},{48,56},{1,9},{9,17},... | collective-permute-start | bytes 49160 | tf_op jit(solution)/shard_map/ppermute | solution.py:22
  248.3 7.5 copy-start.13
  278.1 373.3 %all-gather.2.cloned.1.call-start = ((), (), s32[]{:S(2)}) async-start(), calls=%async_computation.1 | async-start | bytes 5013504 | tf_op jit(solution)/shard_map/all_gather | solution.py:149
  402.2 17.1 %collective-permute-start.7 = (bf16[12,1,1024]{2,1,0:T(2,128)(2,1)S(1)}, bf16[12,1,1024]{2,1,0:T(2,128)(2,1)S(1)}, u32[]{:S(2)}, u32[]{:S(2)}) collective-permute-start(bf16[12,1,1024]{2,1,0:T(2,128)(2,1)S(1)} %get-tuple-element.23), channel_id=1, source_target_pairs={{8,0},{16,8},{24,16},{32,24},{40,32},{48,40},{56,48},{9,1},{17,9},... | collective-permute-start | bytes 73736 | tf_op jit(solution)/shard_map/ppermute | solution.py:23
  403.5 15.8 %collective-permute-start.6 = (bf16[12,1,1024]{2,1,0:T(2,128)(2,1)S(1)}, bf16[12,1,1024]{2,1,0:T(2,128)(2,1)S(1)}, u32[]{:S(2)}, u32[]{:S(2)}) collective-permute-start(bf16[12,1,1024]{2,1,0:T(2,128)(2,1)S(1)} %get-tuple-element.22), channel_id=1, source_target_pairs={{0,8},{8,16},{16,24},{24,32},{32,40},{40,48},{48,56},{1,9},{9,17},... | collective-permute-start | bytes 73736 | tf_op jit(solution)/shard_map/ppermute | solution.py:22
  449.4 68.4 %collective-permute-start.9 = (bf16[8,1,1024]{2,0,1:T(8,128)(2,1)S(1)}, bf16[8,1,1024]{2,0,1:T(8,128)(2,1)S(1)}, u32[]{:S(2)}, u32[]{:S(2)}) collective-permute-start(bf16[8,1,1024]{2,0,1:T(8,128)(2,1)S(1)} %get-tuple-element.31), channel_id=1, source_target_pairs={{8,0},{16,8},{24,16},{32,24},{40,32},{48,40},{56,48},{9,1},{17,9},... | collective-permute-start | bytes 49160 | tf_op jit(solution)/shard_map/ppermute | solution.py:23
  450.7 67.1 %collective-permute-start.8 = (bf16[8,1,1024]{2,0,1:T(8,128)(2,1)S(1)}, bf16[8,1,1024]{2,0,1:T(8,128)(2,1)S(1)}, u32[]{:S(2)}, u32[]{:S(2)}) collective-permute-start(bf16[8,1,1024]{2,0,1:T(8,128)(2,1)S(1)} %get-tuple-element.30), channel_id=1, source_target_pairs={{0,8},{8,16},{16,24},{24,32},{32,40},{40,48},{48,56},{1,9},{9,17},... | collective-permute-start | bytes 49160 | tf_op jit(solution)/shard_map/ppermute | solution.py:22
  472.1 21.3 %copy-start.6 = (bf16[8,1,18,1024]{3,0,2,1:T(8,128)(2,1)S(1)}, bf16[8,1,18,1024]{3,0,2,1:T(8,128)(2,1)}, u32[]{:S(2)}) copy-start(bf16[8,1,18,1024]{3,0,2,1:T(8,128)(2,1)} %get-tuple-element.28) | copy-start | bytes 884740
  676.6 14.1 %copy-start.7 = (bf16[3,3,128,128]{2,3,1,0:T(8,128)(2,1)S(1)}, bf16[3,3,128,128]{2,3,1,0:T(8,128)(2,1)}, u32[]{:S(2)}) copy-start(bf16[3,3,128,128]{2,3,1,0:T(8,128)(2,1)} %all_gather.19) | copy-start | bytes 884740
  705.0 7.3 copy-start.5
  705.0 7.3 copy-start.11
  727.1 109.7 %copy-start.1 = (bf16[3,3,12,16]{3,2,1,0:T(8,128)(2,1)S(1)}, bf16[3,3,12,16]{3,2,1,0:T(8,128)(2,1)}, u32[]{:S(2)}) copy-start(bf16[3,3,12,16]{3,2,1,0:T(8,128)(2,1)} %param.14) | copy-start | bytes 10372
Sparse Core Ops, SparseCore 0:
  278.3 120.3 all-reduce.4
  518.7 40.0 all-gather.1
where the time goes:
time: 855 us; the launch traced here: 844 us
  matrix products  255 us (30%)
  local copies, waits for them, and re-layouts  251 us (29%)
  blocking collectives  145 us (17%)
  waiting for transfers between devices  111 us (13%)
  starting transfers between devices  38 us (4%)
  other arithmetic  25.3 us (3%)
  between operations  19.2 us (2%)
    transpose x3, matrix products, kernel_grad(): return jnp.transpose(result_conv, (2, 3, 0, 1))  184 us
    conv_general_dilated x28, local copies, waits for them, and re-layouts, conv_rows(): lax.conv_general_dilated(grid_field[None], kernel, (1, 1), ((0, 0), (1, 1...  147 us
    psum x1, waiting for transfers between devices, shards(): out_full = lax.psum(out_part, ('section', 'chan'))  111 us
    conv_general_dilated x7, matrix products, conv_rows(): lax.conv_general_dilated(grid_field[None], kernel, (1, 1), ((0, 0), (1, 1...  70.3 us
    psum x1, blocking collectives, shards(): lax.psum((grad_parts[0], grad_parts[1], grad_parts[2], grad_parts[3]), 'r...  43.7 us
    ppermute x5, starting transfers between devices, padded(): before = lax.ppermute(last, axis, up)  31.5 us
    unnamed x1, blocking collectives  30.4 us
    broadcast_in_dim x3, local copies, waits for them, and re-layouts, kernel_grad(): grid_field[:, None]  29 us
  transfers between devices with their start and end apart: 12, of which 1 were waited for; matrix products, arithmetic and copies ran while one was open for 30% of the time, Pallas kernels for 0%

commit v1 on v0

--- a/solution.py
+++ b/solution.py
@@ -131,7 +131,8 @@
     second_hidden = jax.nn.silu(second_act).astype(jnp.bfloat16)
     second_rim = padded(second_hidden, (("rows", 1),), 1)
     out_part = conv_rows(second_rim, third_kernel)
-    out_full = lax.psum(out_part, ("section", "chan"))
+    inner = lax.psum(out_part, "section")
+    out_full = lax.psum(inner, "chan")
     den_value = skip_coef * noisy_field + out_coef * out_full
     out_delta = (2.0 * loss_weight * out_coef * grad_scale * (den_value - resid_field)).astype(
         jnp.bfloat16

time: 855 us -> 802 us (0.938)
  waiting for transfers between devices: 111 us -> 57.2 us
    psum x1 -> x2, waiting for transfers between devices: 111 us -> 55.7 us  [the longest x1 55.7 us: shards(): out_full = lax.psum(inner, 'chan')]
  transfers between devices with their start and end apart: 12 -> 13, of which waited for: 1 -> 2; matrix products, arithmetic and copies ran while one was open for 30% -> 32% of each run, Pallas kernels for 0% -> 0%
where the time goes in v1:
time: 802 us; the launch traced here: 791 us
  matrix products  255 us (32%)
  local copies, waits for them, and re-layouts  251 us (31%)
  blocking collectives  145 us (18%)
  waiting for transfers between devices  57.2 us (7%)
  starting transfers between devices  38.8 us (5%)
  other arithmetic  24.4 us (3%)
  between operations  18.9 us (2%)
    transpose x3, matrix products, kernel_grad(): return jnp.transpose(result_conv, (2, 3, 0, 1))  184 us
    conv_general_dilated x28, local copies, waits for them, and re-layouts, conv_rows(): lax.conv_general_dilated(grid_field[None], kernel, (1, 1), ((0, 0), (1, 1...  147 us
    conv_general_dilated x7, matrix products, conv_rows(): lax.conv_general_dilated(grid_field[None], kernel, (1, 1), ((0, 0), (1, 1...  70.5 us
    psum x1, waiting for transfers between devices, shards(): out_full = lax.psum(inner, 'chan')  55.7 us
    psum x1, blocking collectives, shards(): lax.psum((grad_parts[0], grad_parts[1], grad_parts[2], grad_parts[3]), 'r...  43.9 us
    ppermute x5, starting transfers between devices, padded(): before = lax.ppermute(last, axis, up)  32.2 us
    unnamed x1, blocking collectives  30.4 us
    broadcast_in_dim x3, local copies, waits for them, and re-layouts, kernel_grad(): grid_field[:, None]  29 us
  transfers between devices with their start and end apart: 13, of which 2 were waited for; matrix products, arithmetic and copies ran while one was open for 32% of the time, Pallas kernels for 0%

profile of v1, /device:TPU:0, one launch (start us, length us, event | category | flops | bytes accessed | tf_op | source)
XLA Modules:
  0.0 791.0 jit_solution(14595186192358703844)
XLA Ops:
  18.9 30.4 %all-reduce = bf16[128]{0:T(256)(128)(2,1)S(1)} all-reduce(bf16[128]{0:T(256)(128)(2,1)S(1)} %dynamic-update-slice), channel_id=1, replica_groups=mesh['section'=2,'rows'=8,'chan'=8] {'section','chan'}, use_global_device_ids=true, to_apply=%add | all-reduce | flops 128 | bytes 512
  57.3 7.3 select_bitcast_fusion.1
  74.2 27.6 %all-reduce.9 = bf16[12,8,1024]{2,1,0:T(8,128)(2,1)S(1)} all-reduce(f32[12,8,1024]{2,1,0:T(8,128)S(1)} %slice_bitcast_fusion.3), channel_id=1, replica_groups=mesh['section'=2,'rows'=8,'chan'=8] {'chan'}, use_global_device_ids=true, to_apply=%region_1.2 | all-reduce | flops 98304 | bytes 589824 | tf_op jit(solution)/shard_map/psum | solution.py:112
  111.6 7.0 collective-permute-start.2
  118.6 18.4 %all_gather.16 = bf16[3,3,24,128]{2,3,1,0:T(8,128)(2,1)S(1)} all-gather(bf16[3,3,24,8]{2,3,1,0:T(8,128)(2,1)S(1)} %copy-done.8), channel_id=1, replica_groups=mesh['section'=2,'rows'=8,'chan'=8] {'section','chan'}, dimensions={3}, use_global_device_ids=true | all-gather | bytes 58752 | tf_op jit(solution)/shard_map/all_gather | solution.py:121
  149.7 8.9 %broadcast_select_fusion = f32[18,8,129,128]{3,1,2,0:T(8,128)S(1)} fusion(pred[8,129]{0,1:T(8,128)(4,1)S(1)} %copy-done.10, bf16[3,3,24,128]{2,3,1,0:T(8,128)(2,1)S(1)} %all_gather.16, bf16[24,20,1,7,2]{0,3,4,1,2:T(8,128)(2,1)S(1)} %slice.71, bf16[24,20,1,8,129]{0,3,4,1,2:T(8,128)(2,1)} %copy.92), kind=kOutput, calls=%fused_computation.56 | convolution fusion | flops 1032574464 | bytes 10571400 | tf_op jit(solution)/shard_map/conv_general_dilated | solution.py:45
  162.5 12.6 %fusion.30 = f32[16,8,129,8]{3,1,2,0:T(8,128)} fusion(bf16[3,3,128,8]{2,3,1,0:T(8,128)(2,1)S(1)} %copy-done.9, bf16[18,1,7,1,128]{4,2,3,0,1:T(8,128)(2,1)S(1)} %get-tuple-element.17, bf16[18,1,7,1,128]{4,2,3,0,1:T(8,128)(2,1)S(1)} %get-tuple-element.16, bf16[18,1,8,129,128]{4,2,3,0,1:T(8,128)(2,1)S(1)} %select_bitcast_fusion), kind=kOutput, calls=%fused_computation.39 | convolution fusion | flops 328495104 | bytes 5366784 | tf_op jit(solution)/shard_map/conv_general_dilated | solution.py:45
  183.9 7.3 collective-permute-start.4
  200.4 11.2 %broadcast_select_fusion.3 = f32[16,8,129,12]{3,1,2,0:T(8,128)} fusion(pred[8,129]{0,1:T(8,128)(4,1)S(1)} %copy-done.10, bf16[3,3,8,12]{3,2,1,0:T(8,128)(2,1)S(1)} %copy-done.13, bf16[8,18,1,7,2]{0,3,4,1,2:T(8,128)(2,1)S(1)} %slice.77, bf16[8,18,1,8,129]{0,3,4,1,2:T(8,128)(2,1)} %copy.95), kind=kOutput, calls=%fused_computation.59 | convolution fusion | flops 29636352 | bytes 1096584 | tf_op jit(solution)/shard_map/conv_general_dilated | solution.py:45
  211.6 8.1 %copy.96 = f32[16,8,129,12]{2,1,0,3:T(8,128)} copy(f32[16,8,129,12]{3,1,2,0:T(8,128)} %broadcast_select_fusion.3) | data formatting | bytes 1585152 | tf_op jit(solution)/shard_map/conv_general_dilated | solution.py:45
  223.6 18.9 %all_gather.19 = bf16[3,3,128,128]{2,3,1,0:T(8,128)(2,1)} all-gather(bf16[3,3,128,8]{2,3,1,0:T(8,128)(2,1)S(1)} %copy-done.9), channel_id=1, replica_groups=mesh['section'=2,'rows'=8,'chan'=8] {'section','chan'}, dimensions={3}, use_global_device_ids=true | all-gather | bytes 313344 | tf_op jit(solution)/shard_map/all_gather | solution.py:147
  243.0 18.8 %copy.120 = f32[18,8,129,128]{2,1,3,0:T(8,128)} copy(f32[18,8,129,128]{3,1,2,0:T(8,128)} %copy-done.2) | data formatting | bytes 19021824 | tf_op jit(solution)/shard_map/conv_general_dilated | solution.py:45
  261.8 17.9 %reshape.184 = f32[18,1,1032,128]{2,3,0,1:T(8,128)} reshape(f32[18,8,129,128]{2,1,3,0:T(8,128)} %copy.120) | data formatting | bytes 19021824 | tf_op jit(solution)/shard_map/conv_general_dilated | solution.py:45
  279.8 8.2 %select_convert_fusion.1 = bf16[128,1,18,1024]{3,0,2,1:T(8,128)(2,1)} fusion(f32[128]{0:T(128)S(1)} %multiply_add_fusion.3, pred[18]{0:T(512)(128)(4,1)S(1)} %compare_and_fusion, f32[18,1,1032,128]{2,3,0,1:T(8,128)} %reshape.184), kind=kLoop, calls=%fused_computation.14 | loop fusion | flops 16515072 | bytes 14156306 | tf_op jit(solution)/shard_map/convert_element_type | solution.py:126
  288.6 55.7 %all-reduce.8.cloned.1.call-done = f32[12,16,1024]{2,1,0:T(8,128)} async-done(((f32[12,16,1024]{2,1,0:T(8,128)}), f32[12,16,1024]{2,1,0:T(8,128)}) %all-reduce.8.cloned.1.call-update) | async-done | bytes 786448 | tf_op jit(solution)/shard_map/psum | solution.py:135
  356.1 9.3 %slice.88 = f32[18,1,1024,128]{2,3,0,1:T(8,128)} slice(f32[18,1,1032,128]{2,3,0,1:T(8,128)} %reshape.184), slice={[0:18], [0:1], [0:1024], [0:128]} | slice | bytes 18874368 | tf_op jit(solution)/shard_map/conv_general_dilated | solution.py:45
  375.2 11.1 %broadcast_select_fusion.2 = f32[16,8,129,8]{3,1,2,0:T(8,128)} fusion(pred[8,129]{0,1:T(8,128)(4,1)S(1)} %copy-done.10, bf16[3,3,8,12]{3,2,1,0:T(8,128)(2,1)S(1)} %copy-done.13, bf16[12,18,1,7,2]{0,3,4,1,2:T(8,128)(2,1)S(1)} %slice.82, bf16[12,18,1,8,129]{0,3,4,1,2:T(8,128)(2,1)} %copy.99), kind=kOutput, calls=%fused_computation.58 | convolution fusion | flops 30023040 | bytes 983016 | tf_op jit(solution)/shard_map/conv_general_dilated | solution.py:45
  386.3 7.5 copy.100
  405.3 13.0 %copy.108 = bf16[24,1,18,1024]{0,1,3,2:T(2,128)(2,1)} copy(bf16[24,1,18,1024]{3,2,0,1:T(8,128)(2,1)S(1)} %slice_bitcast_fusion) | data formatting | bytes 1769472 | tf_op jit(solution)/shard_map/broadcast_in_dim | solution.py:58
  418.4 21.4 %copy.110 = bf16[128,1,18,1024]{0,1,3,2:T(2,128)(2,1)} copy(bf16[128,1,18,1024]{3,0,2,1:T(8,128)(2,1)} %select_convert_fusion.1) | data formatting | bytes 9437184 | tf_op jit(solution)/shard_map/convert_element_type | solution.py:126
  439.8 15.5 %copy.112 = bf16[8,1,18,1024]{0,1,3,2:T(2,128)(2,1)} copy(bf16[8,1,18,1024]{3,0,2,1:T(8,128)(2,1)S(1)} %copy-done.6) | data formatting | bytes 589824 | tf_op jit(solution)/shard_map/broadcast_in_dim | solution.py:58
  455.3 9.3 %copy.113 = bf16[12,1,16,1024]{0,1,3,2:T(2,128)(2,1)} copy(bf16[12,1,16,1024]{3,2,0,1:T(8,128)(2,1)S(1)} %bitcast.183) | data formatting | bytes 786432 | tf_op jit(solution)/shard_map/broadcast_in_dim | solution.py:59
  465.4 52.5 %fusion.140 = f32[3,3,8,12]{3,2,1,0:T(8,128)S(1)} fusion(bf16[8,1,18,1024]{0,1,3,2:T(2,128)(2,1)} %copy.112, bf16[12,1,16,1024]{0,1,3,2:T(2,128)(2,1)} %copy.113), kind=kOutput, calls=%fused_computation.171 | convolution fusion | flops 28293120 | bytes 691584 | tf_op jit(solution)/shard_map/transpose | solution.py:65
  518.1 14.3 %copy.111 = bf16[8,1,16,1024]{0,1,3,2:T(2,128)(2,1)} copy(bf16[8,1,16,1024]{3,0,2,1:T(8,128)(2,1)S(1)} %fusion.84) | data formatting | bytes 524288 | tf_op jit(solution)/shard_map/convert_element_type | solution.py:142
  532.4 66.0 %fusion.139 = f32[3,3,128,8]{2,3,1,0:T(8,128)S(1)} fusion(bf16[128,1,18,1024]{0,1,3,2:T(2,128)(2,1)} %copy.110, bf16[8,1,16,1024]{0,1,3,2:T(2,128)(2,1)} %copy.111), kind=kOutput, calls=%fused_computation.170 | convolution fusion | flops 301793280 | bytes 5017600 | tf_op jit(solution)/shard_map/transpose | solution.py:65
  598.3 7.7 pad.12
  606.0 17.5 %reshape.183 = bf16[128,18,1,8,129]{4,3,0,1,2:T(8,128)(2,1)} reshape(bf16[128,18,1,1032]{3,0,1,2:T(8,128)(2,1)} %pad.12) | data formatting | bytes 9510912 | tf_op jit(solution)/shard_map/conv_general_dilated | solution.py:45
  623.4 13.1 %copy.103 = bf16[128,18,1,8,129]{0,3,4,1,2:T(8,128)(2,1)} copy(bf16[128,18,1,8,129]{4,3,0,1,2:T(8,128)(2,1)} %reshape.183) | data formatting | bytes 9510912 | tf_op jit(solution)/shard_map/conv_general_dilated | solution.py:45
  637.5 14.4 %broadcast_select_fusion.1 = f32[16,8,129,8]{3,1,2,0:T(8,128)} fusion(pred[8,129]{0,1:T(8,128)(4,1)S(1)} %copy-done.10, bf16[128,18,1,7,2]{0,3,4,1,2:T(8,128)(2,1)S(1)} %slice.86, bf16[128,18,1,8,129]{0,3,4,1,2:T(8,128)(2,1)} %copy.103, bf16[3,3,128,128]{2,3,1,0:T(8,128)(2,1)S(1)} %copy-done.7, s32[]{:T(128)S(6)} %select_n.34), kind=kOutput, calls=%fused_computation.57 | convolution fusion | flops 318968832 | bytes 5644300 | tf_op jit(solution)/shard_map/conv_general_dilated | solution.py:45
  659.9 14.2 %copy.109 = bf16[8,1,16,1024]{0,1,3,2:T(2,128)(2,1)} copy(bf16[8,1,16,1024]{3,0,2,1:T(8,128)(2,1)S(1)} %fusion.101) | data formatting | bytes 524288 | tf_op jit(solution)/shard_map/broadcast_in_dim | solution.py:59
  674.1 66.0 %fusion.138 = f32[3,3,24,8]{2,3,1,0:T(8,128)S(1)} fusion(bf16[24,1,18,1024]{0,1,3,2:T(2,128)(2,1)} %copy.108, bf16[8,1,16,1024]{0,1,3,2:T(2,128)(2,1)} %copy.109), kind=kOutput, calls=%fused_computation.169 | convolution fusion | flops 56586240 | bytes 1153792 | tf_op jit(solution)/shard_map/transpose | solution.py:65
  740.1 43.9 %all-reduce.1 = (f32[3,3,24,8]{2,3,1,0:T(8,128)}, f32[3,3,128,8]{2,3,1,0:T(8,128)}, f32[3,3,8,12]{3,2,1,0:T(8,128)}, f32[8]{0:T(128)}) all-reduce(f32[3,3,24,8]{2,3,1,0:T(8,128)S(1)} %fusion.138, f32[3,3,128,8]{2,3,1,0:T(8,128)S(1)} %fusion.139, ...), channel_id=1, replica_groups=mesh['section'=2,'rows'=8,'chan'=8] {'rows'}, use_global_device_ids=true, to_apply=%region_4.5 | all-reduce | flops 11816 | bytes 94528 | tf_op jit(solution)/shard_map/psum | solution.py:160
  (118 shorter events, 117.0 us)
Async XLA Ops:
  7.2 50.1 %copy-start = (bf16[3,3,12,16]{3,2,1,0:T(8,128)(2,1)S(1)}, bf16[3,3,12,16]{3,2,1,0:T(8,128)(2,1)}, u32[]{:S(2)}) copy-start(bf16[3,3,12,16]{3,2,1,0:T(8,128)(2,1)} %param.14) | copy-start | bytes 10372
  7.2 50.1 %copy-start.10 = (pred[8,129]{0,1:T(8,128)(4,1)S(1)}, pred[8,129]{0,1:T(8,128)(4,1)}, u32[]{:S(2)}) copy-start(pred[8,129]{0,1:T(8,128)(4,1)} %constant.100) | copy-start | bytes 3100
  7.2 272.5 %all-reduce.6.cloned.1.call-start = ((), (), s32[]{:S(2)}) async-start(), calls=%async_computation | async-start | bytes 1572864 | tf_op jit(solution)/shard_map/psum | solution.py:134
  8.5 42.8 %collective-permute-start = (bf16[12,2,1024]{2,1,0:T(2,128)(2,1)S(1)}, bf16[12,2,1024]{2,1,0:T(2,128)(2,1)S(1)}, u32[]{:S(2)}, u32[]{:S(2)}) collective-permute-start(bf16[12,2,1024]{2,1,0:T(2,128)(2,1)S(1)} %get-tuple-element.26), channel_id=1, source_target_pairs={{0,8},{8,16},{16,24},{24,32},{32,40},{40,48},{48,56},{1,9},{9,17},... | collective-permute-start | bytes 147464 | tf_op jit(solution)/shard_map/ppermute | solution.py:22
  13.5 37.8 %collective-permute-start.1 = (bf16[12,2,1024]{2,1,0:T(2,128)(2,1)S(1)}, bf16[12,2,1024]{2,1,0:T(2,128)(2,1)S(1)}, u32[]{:S(2)}, u32[]{:S(2)}) collective-permute-start(bf16[12,2,1024]{2,1,0:T(2,128)(2,1)S(1)} %get-tuple-element.27), channel_id=1, source_target_pairs={{8,0},{16,8},{24,16},{32,24},{40,32},{48,40},{56,48},{9,1},{17,9},... | collective-permute-start | bytes 147464 | tf_op jit(solution)/shard_map/ppermute | solution.py:23
  57.3 7.4 copy-start.12
  69.6 38.6 %copy-start.4 = (f32[12,16,1024]{2,1,0:T(8,128)S(1)}, f32[12,16,1024]{2,1,0:T(8,128)}, u32[]{:S(2)}) copy-start(f32[12,16,1024]{2,1,0:T(8,128)} %param.11) | copy-start | bytes 2359300
  69.6 49.0 %copy-start.8 = (bf16[3,3,24,8]{2,3,1,0:T(8,128)(2,1)S(1)}, bf16[3,3,24,8]{2,3,1,0:T(8,128)(2,1)}, u32[]{:S(2)}) copy-start(bf16[3,3,24,8]{2,3,1,0:T(8,128)(2,1)} %param.16) | copy-start | bytes 10372
  108.2 28.8 %copy-start.3 = (bf16[12,16,1024]{2,1,0:T(8,128)(2,1)}, bf16[12,16,1024]{2,1,0:T(8,128)(2,1)S(1)}, u32[]{:S(2)}) copy-start(bf16[12,16,1024]{2,1,0:T(8,128)(2,1)S(1)} %all_gather.15) | copy-start | bytes 1179652
  110.3 26.7 %collective-permute-start.3 = (bf16[12,2,1024]{2,1,0:T(2,128)(2,1)S(1)}, bf16[12,2,1024]{2,1,0:T(2,128)(2,1)S(1)}, u32[]{:S(2)}, u32[]{:S(2)}) collective-permute-start(bf16[12,2,1024]{2,1,0:T(2,128)(2,1)S(1)} %get-tuple-element.25), channel_id=1, source_target_pairs={{8,0},{16,8},{24,16},{32,24},{40,32},{48,40},{56,48},{9,1},{17,9},... | collective-permute-start | bytes 147464 | tf_op jit(solution)/shard_map/ppermute | solution.py:23
  111.6 25.4 %collective-permute-start.2 = (bf16[12,2,1024]{2,1,0:T(2,128)(2,1)S(1)}, bf16[12,2,1024]{2,1,0:T(2,128)(2,1)S(1)}, u32[]{:S(2)}, u32[]{:S(2)}) collective-permute-start(bf16[12,2,1024]{2,1,0:T(2,128)(2,1)S(1)} %get-tuple-element.24), channel_id=1, source_target_pairs={{0,8},{8,16},{16,24},{24,32},{32,40},{40,48},{48,56},{1,9},{9,17},... | collective-permute-start | bytes 147464 | tf_op jit(solution)/shard_map/ppermute | solution.py:22
  158.6 3.9 copy-start.2
  158.6 3.9 copy-start.9
  182.0 18.4 %copy-start.13 = (bf16[3,3,8,12]{3,2,1,0:T(8,128)(2,1)S(1)}, bf16[3,3,8,12]{3,2,1,0:T(8,128)(2,1)}, u32[]{:S(2)}) copy-start(bf16[3,3,8,12]{3,2,1,0:T(8,128)(2,1)} %param.18) | copy-start | bytes 5188
  182.6 8.6 %collective-permute-start.5 = (bf16[8,1,1024]{2,0,1:T(8,128)(2,1)S(1)}, bf16[8,1,1024]{2,0,1:T(8,128)(2,1)S(1)}, u32[]{:S(2)}, u32[]{:S(2)}) collective-permute-start(bf16[8,1,1024]{2,0,1:T(8,128)(2,1)S(1)} %get-tuple-element.33), channel_id=1, source_target_pairs={{8,0},{16,8},{24,16},{32,24},{40,32},{48,40},{56,48},{9,1},{17,9},... | collective-permute-start | bytes 49160 | tf_op jit(solution)/shard_map/ppermute | solution.py:23
  183.9 8.7 %collective-permute-start.4 = (bf16[8,1,1024]{2,0,1:T(8,128)(2,1)S(1)}, bf16[8,1,1024]{2,0,1:T(8,128)(2,1)S(1)}, u32[]{:S(2)}, u32[]{:S(2)}) collective-permute-start(bf16[8,1,1024]{2,0,1:T(8,128)(2,1)S(1)} %get-tuple-element.32), channel_id=1, source_target_pairs={{0,8},{8,16},{16,24},{24,32},{32,40},{40,48},{48,56},{1,9},{9,17},... | collective-permute-start | bytes 49160 | tf_op jit(solution)/shard_map/ppermute | solution.py:22
  219.6 22.8 %copy-start.14 = (bf16[8]{0:T(256)(128)(2,1)S(1)}, bf16[8]{0:T(256)(128)(2,1)}, u32[]{:S(2)}) copy-start(bf16[8]{0:T(256)(128)(2,1)} %param.19) | copy-start | bytes 52
  222.7 121.6 %all-reduce.8.cloned.1.call-start = ((), (), s32[]{:S(2)}) async-start(), calls=%async_computation.1 | async-start | bytes 1572864 | tf_op jit(solution)/shard_map/psum | solution.py:135
  279.7 318.6 %all-gather.2.cloned.1.call-start = ((), (), s32[]{:S(2)}) async-start(), calls=%async_computation.2 | async-start | bytes 5013504 | tf_op jit(solution)/shard_map/all_gather | solution.py:150
  347.9 17.5 %collective-permute-start.7 = (bf16[12,1,1024]{2,1,0:T(2,128)(2,1)S(1)}, bf16[12,1,1024]{2,1,0:T(2,128)(2,1)S(1)}, u32[]{:S(2)}, u32[]{:S(2)}) collective-permute-start(bf16[12,1,1024]{2,1,0:T(2,128)(2,1)S(1)} %get-tuple-element.23), channel_id=1, source_target_pairs={{8,0},{16,8},{24,16},{32,24},{40,32},{48,40},{56,48},{9,1},{17,9},... | collective-permute-start | bytes 73736 | tf_op jit(solution)/shard_map/ppermute | solution.py:23
  349.2 16.2 %collective-permute-start.6 = (bf16[12,1,1024]{2,1,0:T(2,128)(2,1)S(1)}, bf16[12,1,1024]{2,1,0:T(2,128)(2,1)S(1)}, u32[]{:S(2)}, u32[]{:S(2)}) collective-permute-start(bf16[12,1,1024]{2,1,0:T(2,128)(2,1)S(1)} %get-tuple-element.22), channel_id=1, source_target_pairs={{0,8},{8,16},{16,24},{24,32},{32,40},{40,48},{48,56},{1,9},{9,17},... | collective-permute-start | bytes 73736 | tf_op jit(solution)/shard_map/ppermute | solution.py:22
  395.6 69.0 %collective-permute-start.9 = (bf16[8,1,1024]{2,0,1:T(8,128)(2,1)S(1)}, bf16[8,1,1024]{2,0,1:T(8,128)(2,1)S(1)}, u32[]{:S(2)}, u32[]{:S(2)}) collective-permute-start(bf16[8,1,1024]{2,0,1:T(8,128)(2,1)S(1)} %get-tuple-element.31), channel_id=1, source_target_pairs={{8,0},{16,8},{24,16},{32,24},{40,32},{48,40},{56,48},{9,1},{17,9},... | collective-permute-start | bytes 49160 | tf_op jit(solution)/shard_map/ppermute | solution.py:23
  396.9 67.7 %collective-permute-start.8 = (bf16[8,1,1024]{2,0,1:T(8,128)(2,1)S(1)}, bf16[8,1,1024]{2,0,1:T(8,128)(2,1)S(1)}, u32[]{:S(2)}, u32[]{:S(2)}) collective-permute-start(bf16[8,1,1024]{2,0,1:T(8,128)(2,1)S(1)} %get-tuple-element.30), channel_id=1, source_target_pairs={{0,8},{8,16},{16,24},{24,32},{32,40},{40,48},{48,56},{1,9},{9,17},... | collective-permute-start | bytes 49160 | tf_op jit(solution)/shard_map/ppermute | solution.py:22
  418.4 21.4 %copy-start.6 = (bf16[8,1,18,1024]{3,0,2,1:T(8,128)(2,1)S(1)}, bf16[8,1,18,1024]{3,0,2,1:T(8,128)(2,1)}, u32[]{:S(2)}) copy-start(bf16[8,1,18,1024]{3,0,2,1:T(8,128)(2,1)} %get-tuple-element.28) | copy-start | bytes 884740
  623.4 14.1 %copy-start.7 = (bf16[3,3,128,128]{2,3,1,0:T(8,128)(2,1)S(1)}, bf16[3,3,128,128]{2,3,1,0:T(8,128)(2,1)}, u32[]{:S(2)}) copy-start(bf16[3,3,128,128]{2,3,1,0:T(8,128)(2,1)} %all_gather.19) | copy-start | bytes 884740
  651.9 7.3 copy-start.5
  652.0 7.3 copy-start.11
  674.1 109.9 %copy-start.1 = (bf16[3,3,12,16]{3,2,1,0:T(8,128)(2,1)S(1)}, bf16[3,3,12,16]{3,2,1,0:T(8,128)(2,1)}, u32[]{:S(2)}) copy-start(bf16[3,3,12,16]{3,2,1,0:T(8,128)(2,1)} %param.14) | copy-start | bytes 10372
Sparse Core Ops, SparseCore 0:
  222.9 42.4 all-reduce.5
  279.8 64.4 all-reduce.7
  465.5 38.5 all-gather.1
